TPU v7x, 32 devices: a whole 2x2x4 slice. The times are simulated.
32 devices in a mesh: req: 8 (over y, x, core), blk: 4 (over z).
Axes of the slice: x: 2, y: 2, z: 4, core: 2. Of those that a mesh axis runs over, the one named last changes fastest.
Arguments:
- x_img: bfloat16 [8, 1024, 1536], P('req', 'blk'), may hold values from -0.3 to 0.3
- x_txt: bfloat16 [8, 154, 1536], P('req'), may hold values from -6 to 6
- modulation: float32 [8, 7, 1536], P('req'), may hold values from -8 to 8
- w_img: bfloat16 [1536, 2304], P(None, 'req'), may hold values from -0.375 to 0.375
- w_txt: bfloat16 [1536, 1536], P(None, 'req'), may hold values from -0.15625 to 0.15625
- w_out: bfloat16 [768, 1536], P('req'), may hold values from -0.21875 to 0.21875
- w_final: bfloat16 [1536, 64], replicated, may hold values from -0.15625 to 0.15625
- lengths: int32 [8], P('req'), may hold values from 16 to 154, as said below
- block_mask: int32 [8, 4, 4], P('req', 'blk'), may hold values from 0 to 1, as said below
- timestep: int32 [8], P('req'), may hold values from 0 to 27
- latent: float32 [8, 16, 32, 128], P('req', None, 'blk'), may hold values from -6 to 6
- conv_w: bfloat16 [512, 144], replicated, may hold values from -0.5 to 0.5
Outputs:
- velocity: float32 [8, 16, 32, 128], P('req', None, 'blk')
- latent_next: float32 [8, 16, 32, 128], P('req', None, 'blk')
- features: bfloat16 [8, 512, 32, 128], P('req', None, 'blk')
Inputs may be any that keep to these rules, and one draw needn't show every extreme that they name: Text keys from position lengths[r] on are padding; some request uses all 154 text tokens. Every tile may attend to its own keys: block_mask[r, t, t] = 1.
All inputs are finite; a program needn't handle non-finite values.
Results may differ from a plain program's by a relative error of at most 0.0063.
Values may be sent and summed in bfloat16 or wider, within the bound.
A program may use at most 192 MiB of HBM per device.

v0:
```python
import jax
import jax.numpy as jnp
from jax import lax
from jax.sharding import PartitionSpec as P

HD = 64
GRIDW = 64
PATCH = 2
LATC = 16
NSTEPS = 28
NORM_EPS = 1e-06
SHIFT_FACTOR = 3.0
LATENT_SCALE = 1.5305
LATENT_SHIFT = 0.0609
NEG_LARGE = -1e30
SCORE_SCALE = 0.125


def with_halo(block, sides, width):
    for axis, dim in sides:
        count = lax.axis_size(axis)
        forward = [(i, i + 1) for i in range(count - 1)]
        backward = [(target, source) for source, target in forward]
        low = lax.ppermute(
            lax.slice_in_dim(block, block.shape[dim] - width, None, axis=dim), axis, forward
        )
        high = lax.ppermute(lax.slice_in_dim(block, 0, width, axis=dim), axis, backward)
        block = jnp.concatenate([low, block, high], axis=dim)
    return block


def layer_norm(values):
    values = values.astype(jnp.float32)
    center = values - jnp.mean(values, axis=-1, keepdims=True)
    spread = jnp.mean(center * center, axis=-1, keepdims=True)
    return center * lax.rsqrt(spread + NORM_EPS)


def modulate(values, shift_row, scale_row):
    return layer_norm(values) * (1.0 + scale_row) + shift_row


def sigma_of(step_index, step_count):
    fraction = 1.0 - step_index.astype(jnp.float32) / step_count
    return SHIFT_FACTOR * fraction / (1.0 + (SHIFT_FACTOR - 1.0) * fraction)


def unpatchify(token_out, grid_width, patch_size, channels):
    patch_rows = token_out.shape[0] // grid_width
    shaped = token_out.reshape(patch_rows, grid_width, patch_size, patch_size, channels)
    shaped = jnp.transpose(shaped, (4, 0, 2, 1, 3))
    return shaped.reshape(channels, patch_rows * patch_size, grid_width * patch_size)


def convolve(padded, conv_w):
    row_count = padded.shape[1] - 2
    col_count = padded.shape[2] - 2
    tap_list = [
        padded[:, tap_row : tap_row + row_count, tap_col : tap_col + col_count]
        for tap_row in range(3)
        for tap_col in range(3)
    ]
    stacked = jnp.stack(tap_list, axis=1).reshape(padded.shape[0] * 9, row_count * col_count)
    convolved = jnp.dot(conv_w, stacked, preferred_element_type=jnp.float32)
    return convolved.reshape(conv_w.shape[0], row_count, col_count)


def text_state(queries, keys_txt, vals_txt, length):
    text_allowed = (jnp.arange(keys_txt.shape[0], dtype=jnp.int32) < length)[None, None, :]
    text_scores = (
        jnp.einsum("qhd,khd->qhk", queries, keys_txt, preferred_element_type=jnp.float32)
        * SCORE_SCALE
    )
    text_scores = jnp.where(text_allowed, text_scores, NEG_LARGE)
    text_max = jnp.max(text_scores, axis=2)
    text_weights = jnp.where(text_allowed, jnp.exp(text_scores - text_max[:, :, None]), 0.0)
    text_acc = jnp.einsum(
        "qhk,khd->qhd",
        text_weights.astype(jnp.bfloat16),
        vals_txt,
        preferred_element_type=jnp.float32,
    )
    return (text_max, jnp.sum(text_weights, axis=2), text_acc)


def absorb_block(previous, queries, head_keys, head_vals, allowed):
    old_max, old_sum, old_acc = previous
    scores = (
        jnp.einsum("qhd,khd->qhk", queries, head_keys, preferred_element_type=jnp.float32)
        * SCORE_SCALE
    )
    scores = jnp.where(allowed, scores, NEG_LARGE)
    new_max = jnp.maximum(old_max, jnp.max(scores, axis=2))
    weights = jnp.where(allowed, jnp.exp(scores - new_max[:, :, None]), 0.0)
    factor = jnp.exp(old_max - new_max)
    summed = jnp.einsum(
        "qhk,khd->qhd", weights.astype(jnp.bfloat16), head_vals, preferred_element_type=jnp.float32
    )
    return (
        new_max,
        old_sum * factor + jnp.sum(weights, axis=2),
        old_acc * factor[:, :, None] + summed,
    )


def absorb_maybe(previous, queries, head_keys, head_vals, allowed):
    return absorb_block(previous, queries, head_keys, head_vals, allowed)


def on_device(
    x_img,
    x_txt,
    modulation,
    w_img,
    w_txt,
    w_out,
    w_final,
    lengths,
    block_mask,
    timestep,
    latent,
    conv_w,
):
    tokens = x_img[0]
    factors = modulation[0]
    tok_rows = tokens.shape[0]
    head_cols = w_out.shape[0] * lax.axis_size("req")
    head_count = head_cols // HD
    h_img = modulate(tokens, factors[0], factors[1]).astype(jnp.bfloat16)
    h_txt = modulate(x_txt[0], factors[3], factors[4]).astype(jnp.bfloat16)
    qkv = jnp.dot(
        h_img, lax.all_gather(w_img, "req", axis=1, tiled=True), preferred_element_type=jnp.float32
    ).astype(jnp.bfloat16)
    kv_txt = jnp.dot(
        h_txt, lax.all_gather(w_txt, "req", axis=1, tiled=True), preferred_element_type=jnp.float32
    ).astype(jnp.bfloat16)
    keys_txt = kv_txt[:, :head_cols].reshape(-1, head_count, HD)
    vals_txt = kv_txt[:, head_cols:].reshape(-1, head_count, HD)
    length = lengths[0]
    queries = qkv[:, :head_cols].reshape(tok_rows, head_count, HD)
    keys_img = qkv[:, head_cols : 2 * head_cols]
    vals_img = qkv[:, 2 * head_cols :]
    mask_row = block_mask[0, 0]
    tile_count = mask_row.shape[0]
    start_state = text_state(queries, keys_txt, vals_txt, length)
    piece_keys = lax.all_gather(keys_img, "blk", axis=0, tiled=True)
    piece_vals = lax.all_gather(vals_img, "blk", axis=0, tiled=True)
    piece_len = piece_keys.shape[0]
    key_tile = jnp.arange(piece_len, dtype=jnp.int32) // tok_rows
    tile_hit = key_tile[:, None] == jnp.arange(tile_count, dtype=jnp.int32)[None, :]
    allowed = jnp.sum(jnp.where(tile_hit, mask_row[None, :], 0), axis=1) == 1
    head_keys = piece_keys.reshape(piece_len, head_count, HD)
    head_vals = piece_vals.reshape(piece_len, head_count, HD)
    run_max, run_sum, run_acc = absorb_maybe(
        start_state, queries, head_keys, head_vals, allowed[None, None, :]
    )
    attended = (run_acc / run_sum[:, :, None]).reshape(tok_rows, head_cols).astype(jnp.bfloat16)
    projected = jnp.dot(
        attended,
        lax.all_gather(w_out, "req", axis=0, tiled=True),
        preferred_element_type=jnp.float32,
    )
    residual = tokens.astype(jnp.float32) + factors[2] * projected
    final_in = modulate(residual, factors[5], factors[6]).astype(jnp.bfloat16)
    token_out = jnp.dot(final_in, w_final, preferred_element_type=jnp.float32)
    velocity = unpatchify(token_out, GRIDW, PATCH, LATC)[None]
    step_index = timestep[0]
    sigma_step = sigma_of(step_index + 1, NSTEPS) - sigma_of(step_index, NSTEPS)
    latent_next = latent + sigma_step * velocity
    decoded = (latent_next / LATENT_SCALE + LATENT_SHIFT).astype(jnp.bfloat16)
    padded = with_halo(decoded, (("blk", 2),), 1)
    padded = jnp.pad(padded[0], ((0, 0), (0, 0), (1, 1)))
    features = convolve(padded, conv_w).astype(jnp.bfloat16)[None]
    return (velocity, latent_next, features)


def solution(mesh):
    return jax.shard_map(
        on_device,
        mesh=mesh,
        in_specs=(
            P("req", "blk", None),
            P("req", None, None),
            P("req", None, None),
            P(None, "req"),
            P(None, "req"),
            P("req", None),
            P(),
            P("req"),
            P("req", "blk", None),
            P("req"),
            P("req", None, "blk", None),
            P(),
        ),
        out_specs=(
            P("req", None, "blk", None),
            P("req", None, "blk", None),
            P("req", None, "blk", None),
        ),
        check_vma=False,
    )
```

profile of v0, /device:TPU:0, one launch (start us, length us, event | category | flops | bytes accessed | tf_op | source)
XLA Modules:
  0.0 230.1 jit_solution(16971153236048344387)
XLA Ops:
  7.2 0.0 copy-start
  7.2 0.0 all-gather.8.cloned.1.call-start
  7.2 0.7 all-gather.8.cloned.1.call-update
  7.9 0.0 all-gather.6.cloned.1.call-start
  8.0 0.7 all-gather.6.cloned.1.call-update
  8.7 0.0 all-gather.10.cloned.1.call-start
  8.7 0.9 add_reduce_fusion
  9.6 0.0 copy-done.2
  9.6 0.2 convert_reduce_fusion
  9.8 0.3 fusion.14
  10.2 51.3 %all-gather.8.cloned.1.call-done = bf16[1536,2304]{0,1:T(8,128)(2,1)} async-done(((bf16[1536,288]{0,1:T(8,128)(2,1)}), bf16[1536,2304]{0,1:T(8,128)(2,1)}) %all-gather.8.cloned.1.call-update) | async-done | bytes 7077904 | tf_op jit(solution)/shard_map/all_gather | solution.py:132
  61.5 5.2 %convolution_convert_fusion = bf16[256,2304]{1,0:T(8,128)(2,1)S(1)} fusion(bf16[1536,2304]{0,1:T(8,128)(2,1)} %all-gather.8.cloned.1.call-done, bf16[1,256,1536]{2,1,0:T(8,128)(2,1)S(1)} %copy-done.2, f32[1536]{0:T(1024)S(1)} %get-tuple-element.16, f32[1536]{0:T(1024)S(1)} %get-tuple-element.17, f32[256]{0:T(256)S(1)} %add_rsqrt_fusion.1, ...), kind=kOutput, calls=%fused_computation.10 | convolution fusion | flops 1814888448 | bytes 9058304 | tf_op jit(solution)/shard_map/dot_general | solution.py:131
  66.7 0.0 copy-start.4
  66.7 0.0 copy-start.8
  66.7 0.0 copy-start.7
  66.7 1.0 fusion.69
  67.7 0.0 all-gather.10.cloned.1.call-update
  67.7 0.0 all-gather.12.cloned.1.call-start
  67.7 0.5 all-gather.12.cloned.1.call-update
  68.3 0.0 all-gather.14.cloned.1.call-start
  68.3 0.5 all-gather.14.cloned.1.call-update
  69.5 0.1 convert_reduce_fusion.1
  69.7 0.3 fusion.30
  70.7 0.0 copy-done.8
  70.7 0.1 select_reduce_fusion
  70.8 1.0 copy.66
  71.9 30.4 %all-gather.6.cloned.1.call-done = bf16[1536,1536]{0,1:T(8,128)(2,1)} async-done(((bf16[1536,192]{0,1:T(8,128)(2,1)}), bf16[1536,1536]{0,1:T(8,128)(2,1)}) %all-gather.6.cloned.1.call-update) | async-done | bytes 4718608 | tf_op jit(solution)/shard_map/all_gather | solution.py:135
  102.3 4.0 %convolution_convert_fusion.1 = bf16[154,1536]{1,0:T(8,128)(2,1)S(1)} fusion(bf16[1536,1536]{0,1:T(8,128)(2,1)} %all-gather.6.cloned.1.call-done, bf16[1,154,1536]{2,1,0:T(8,128)(2,1)S(1)} %copy-done.4, f32[1536]{0:T(1024)S(1)} %get-tuple-element.18, f32[1536]{0:T(1024)S(1)} %get-tuple-element.19, f32[154]{0:T(256)S(1)} %add_rsqrt_fusion.2, ...), kind=kOutput, calls=%fused_computation.13 | convolution fusion | flops 728318976 | bytes 5678288 | tf_op jit(solution)/shard_map/dot_general | solution.py:134
  106.4 0.9 copy.60
  107.3 0.9 copy.59
  108.3 0.2 copy.61
  108.4 1.6 bitcast_reduce_fusion.1
  110.0 0.6 fusion.18
  110.6 30.5 %all-gather.10.cloned.1.call-done = bf16[1024,768]{1,0:T(8,128)(2,1)} async-done(((bf16[256,768]{1,0:T(8,128)(2,1)}), bf16[1024,768]{1,0:T(8,128)(2,1)}) %all-gather.10.cloned.1.call-update) | async-done | bytes 1572880 | tf_op jit(solution)/shard_map/all_gather | solution.py:146
  141.0 2.6 %copy.62 = bf16[1024,768]{0,1:T(8,128)(2,1)} copy(bf16[1024,768]{1,0:T(8,128)(2,1)} %all-gather.10.cloned.1.call-done) | data formatting | bytes 3145728 | tf_op jit(solution)/shard_map/all_gather | solution.py:146
  143.6 8.8 %bitcast_reduce_fusion = (f32[256,12]{0,1:T(8,128)S(1)}, f32[12,1024,256]{2,1,0:T(8,128)}) fusion(pred[1024]{0:T(1024)(128)(4,1)S(1)} %broadcast_compare_fusion, bf16[1024,12,64]{0,2,1:T(8,128)(2,1)} %bitcast.129, bf16[256,12,64]{0,2,1:T(8,128)(2,1)S(1)} %bitcast.134), kind=kOutput, calls=%fused_computation.1 | convolution fusion | flops 412087296 | bytes 14562304 | tf_op jit(solution)/shard_map/qhd,khd->qhk/dot_general | solution.py:89
  152.5 26.0 %all-gather.12.cloned.1.call-done = bf16[1024,768]{1,0:T(8,128)(2,1)} async-done(((bf16[256,768]{1,0:T(8,128)(2,1)}), bf16[1024,768]{1,0:T(8,128)(2,1)}) %all-gather.12.cloned.1.call-update) | async-done | bytes 1572880 | tf_op jit(solution)/shard_map/all_gather | solution.py:147
  178.4 2.6 %copy.63 = bf16[1024,768]{0,1:T(8,128)(2,1)} copy(bf16[1024,768]{1,0:T(8,128)(2,1)} %all-gather.12.cloned.1.call-done) | data formatting | bytes 3145728 | tf_op jit(solution)/shard_map/all_gather | solution.py:147
  181.0 7.2 %fusion.2 = f32[256,12]{0,1:T(8,128)S(1)} fusion(f32[12,1024,256]{2,1,0:T(8,128)} %get-tuple-element.45, f32[256,12]{0,1:T(8,128)S(1)} %max.13, pred[1024]{0:T(1024)(128)(4,1)S(1)} %broadcast_compare_fusion), kind=kLoop, calls=%fused_computation.5 | loop fusion | flops 15725568 | bytes 12608512 | tf_op jit(solution)/shard_map/reduce_sum | solution.py:101
  188.3 1.3 copy-done.1
  189.6 4.3 %fusion.20 = f32[256,12,64]{0,2,1:T(8,128)S(1)} fusion(bf16[1024,12,64]{0,2,1:T(8,128)(2,1)} %bitcast.135, f32[12,1024,256]{2,1,0:T(8,128)S(1)} %copy-done.1, f32[256,12]{0,1:T(8,128)S(1)} %max.13, pred[1024]{0:T(1024)(128)(4,1)S(1)} %broadcast_compare_fusion), kind=kOutput, calls=%fused_computation.33 | convolution fusion | flops 418381824 | bytes 14955520 | tf_op jit(solution)/shard_map/qhk,khd->qhd/dot_general | solution.py:96
  193.9 0.0 copy-done.5
  193.9 0.7 fusion.26
  194.6 13.5 %all-gather.14.cloned.1.call-done = bf16[768,1536]{1,0:T(8,128)(2,1)} async-done(((bf16[96,1536]{1,0:T(8,128)(2,1)}), bf16[768,1536]{1,0:T(8,128)(2,1)}) %all-gather.14.cloned.1.call-update) | async-done | bytes 2359312 | tf_op jit(solution)/shard_map/all_gather | solution.py:160
  208.1 2.5 %fusion.72 = (f32[256]{0:T(256)S(1)}, f32[256,1536]{1,0:T(8,128)S(1)}) fusion(bf16[256,768]{0,1:T(8,128)(2,1)S(1)} %bitcast.137, bf16[768,1536]{1,0:T(8,128)(2,1)} %all-gather.14.cloned.1.call-done, f32[1536]{0:T(1024)S(1)} %get-tuple-element.20, bf16[1,256,1536]{2,1,0:T(8,128)(2,1)S(1)} %copy-done.2), kind=kOutput, calls=%fused_computation.127 | convolution fusion | flops 605552384 | bytes 5118976 | tf_op jit(solution)/shard_map/dot_general | solution.py:158
  210.6 0.0 copy-start.3
  210.6 0.3 multiply_reduce_fusion
  211.0 0.5 fusion.46
  211.4 0.1 reshape.190
  211.6 0.3 copy.65
  211.8 0.0 copy-start.6
  211.9 0.1 add_convert_fusion.2
  212.0 3.4 %collective-permute-start = (bf16[1,16,1,128]{1,3,2,0:T(8,128)(2,1)S(1)}, bf16[1,16,1,128]{1,3,2,0:T(8,128)(2,1)S(1)}, u32[]{:S(2)}, u32[]{:S(2)}) collective-permute-start(bf16[1,16,1,128]{1,3,2,0:T(8,128)(2,1)S(1)} %get-tuple-element.31), channel_id=1, source_target_pairs={{0,1},{1,2},{2,3},{4,5},{5,6},{6,7},{8,9},{9,10},{10,11},{12,13},{... | collective-permute-start | bytes 12296 | tf_op jit(solution)/shard_map/ppermute | solution.py:24
  215.4 1.3 collective-permute-start.1
  216.7 0.1 copy.68
  216.8 0.8 copy.79
  217.6 0.8 copy.80
  218.4 0.0 collective-permute-done
  218.4 0.1 copy.67
  218.5 2.7 %collective-permute-done.1 = bf16[1,16,1,128]{1,3,2,0:T(8,128)(2,1)S(1)} collective-permute-done((bf16[1,16,1,128]{1,3,2,0:T(8,128)(2,1)S(1)}, bf16[1,16,1,128]{1,3,2,0:T(8,128)(2,1)S(1)}, u32[]{:S(2)}, u32[]{:S(2)}) %collective-permute-start.1) | collective-permute-done | bytes 4128 | tf_op jit(solution)/shard_map/ppermute | solution.py:27
  221.2 0.1 copy.69
  221.3 0.1 fusion.59
  221.6 0.5 convolution_convert_fusion.2
  222.1 1.5 copy.81
  (31 shorter events, 0.3 us)
Async XLA Ops:
  7.2 203.8 %copy-start = (bf16[1536,64]{0,1:T(8,128)(2,1)S(1)}, bf16[1536,64]{0,1:T(8,128)(2,1)}, u32[]{:S(2)}) copy-start(bf16[1536,64]{0,1:T(8,128)(2,1)} %param.18) | copy-start | bytes 589828
  7.2 2.5 %copy-start.2 = (bf16[1,256,1536]{2,1,0:T(8,128)(2,1)S(1)}, bf16[1,256,1536]{2,1,0:T(8,128)(2,1)}, u32[]{:S(2)}) copy-start(bf16[1,256,1536]{2,1,0:T(8,128)(2,1)} %param.12) | copy-start | bytes 2359300
  7.2 54.3 %all-gather.8.cloned.1.call-start = ((), (), s32[]{:S(2)}) async-start(), calls=%async_computation.1 | async-start | bytes 7962624 | tf_op jit(solution)/shard_map/all_gather | solution.py:132
  7.9 94.4 %all-gather.6.cloned.1.call-start = ((), (), s32[]{:S(2)}) async-start(), calls=%async_computation | async-start | bytes 5308416 | tf_op jit(solution)/shard_map/all_gather | solution.py:135
  8.7 132.4 %all-gather.10.cloned.1.call-start = ((), (), s32[]{:S(2)}) async-start(), calls=%async_computation.2 | async-start | bytes 1966080 | tf_op jit(solution)/shard_map/all_gather | solution.py:146
  66.7 2.9 %copy-start.4 = (bf16[1,154,1536]{2,1,0:T(8,128)(2,1)S(1)}, bf16[1,154,1536]{2,1,0:T(8,128)(2,1)}, u32[]{:S(2)}) copy-start(bf16[1,154,1536]{2,1,0:T(8,128)(2,1)} %param.13) | copy-start | bytes 1419268
  66.7 4.0 %copy-start.8 = (s32[1,1,4]{2,1,0:T(1,128)S(1)}, s32[1,1,4]{2,1,0:T(1,128)}, u32[]{:S(2)}) copy-start(s32[1,1,4]{2,1,0:T(1,128)} %param.20) | copy-start | bytes 52
  66.7 4.1 %copy-start.7 = (f32[1,16,8,128]{3,2,1,0:T(8,128)S(1)}, f32[1,16,8,128]{3,2,1,0:T(8,128)}, u32[]{:S(2)}) copy-start(f32[1,16,8,128]{3,2,1,0:T(8,128)} %param.22) | copy-start | bytes 196612
  67.7 110.8 %all-gather.12.cloned.1.call-start = ((), (), s32[]{:S(2)}) async-start(), calls=%async_computation.3 | async-start | bytes 1966080 | tf_op jit(solution)/shard_map/all_gather | solution.py:147
  68.3 139.8 %all-gather.14.cloned.1.call-start = ((), (), s32[]{:S(2)}) async-start(), calls=%async_computation.4 | async-start | bytes 2654208 | tf_op jit(solution)/shard_map/all_gather | solution.py:160
  181.0 8.5 %copy-start.1 = (f32[12,1024,256]{2,1,0:T(8,128)S(1)}, f32[12,1024,256]{2,1,0:T(8,128)}, u32[]{:S(2)}) copy-start(f32[12,1024,256]{2,1,0:T(8,128)} %get-tuple-element.45) | copy-start | bytes 37748740
  189.6 4.3 %copy-start.5 = (bf16[154,768]{0,1:T(8,128)(2,1)S(1)}, bf16[154,768]{0,1:T(8,128)(2,1)}, u32[]{:S(2)}) copy-start(bf16[154,768]{0,1:T(8,128)(2,1)} %copy.59) | copy-start | bytes 709636
  210.6 1.2 copy-start.3
  211.8 9.8 %copy-start.6 = (bf16[512,144]{0,1:T(8,128)(2,1)S(1)}, bf16[512,144]{0,1:T(8,128)(2,1)}, u32[]{:S(2)}) copy-start(bf16[512,144]{0,1:T(8,128)(2,1)} %param.23) | copy-start | bytes 442372
  212.0 6.4 %collective-permute-start = (bf16[1,16,1,128]{1,3,2,0:T(8,128)(2,1)S(1)}, bf16[1,16,1,128]{1,3,2,0:T(8,128)(2,1)S(1)}, u32[]{:S(2)}, u32[]{:S(2)}) collective-permute-start(bf16[1,16,1,128]{1,3,2,0:T(8,128)(2,1)S(1)} %get-tuple-element.31), channel_id=1, source_target_pairs={{0,1},{1,2},{2,3},{4,5},{5,6},{6,7},{8,9},{9,10},{10,11},{12,13},{... | collective-permute-start | bytes 12296 | tf_op jit(solution)/shard_map/ppermute | solution.py:24
  215.4 5.8 %collective-permute-start.1 = (bf16[1,16,1,128]{1,3,2,0:T(8,128)(2,1)S(1)}, bf16[1,16,1,128]{1,3,2,0:T(8,128)(2,1)S(1)}, u32[]{:S(2)}, u32[]{:S(2)}) collective-permute-start(bf16[1,16,1,128]{1,3,2,0:T(8,128)(2,1)S(1)} %get-tuple-element.32), channel_id=1, source_target_pairs={{1,0},{2,1},{3,2},{5,4},{6,5},{7,6},{9,8},{10,9},{11,10},{13,12},{... | collective-permute-start | bytes 12296 | tf_op jit(solution)/shard_map/ppermute | solution.py:27
Sparse Core Ops, SparseCore 0:
  9.9 51.5 all-gather.7
  63.4 38.9 all-gather.5
  103.9 37.0 all-gather.9
  142.5 35.9 all-gather.11
  180.2 27.8 all-gather.13
where the time goes:
time: 231 us; the launch traced here: 230 us
  waiting for transfers between devices  157 us (68%)
  matrix products  28 us (12%)
  between operations  15.5 us (7%)
  local copies, waits for them, and re-layouts  14.5 us (6%)
  other arithmetic  10.2 us (4%)
  starting transfers between devices  4.88 us (2%)
    all_gather x1, waiting for transfers between devices, on_device(): lax.all_gather(w_img, 'req', axis=1, tiled=True)  51.3 us
    all_gather x1, waiting for transfers between devices, on_device(): piece_keys = lax.all_gather(keys_img, 'blk', axis=0, tiled=True)  30.5 us
    all_gather x1, waiting for transfers between devices, on_device(): lax.all_gather(w_txt, 'req', axis=1, tiled=True)  30.4 us
    all_gather x1, waiting for transfers between devices, on_device(): piece_vals = lax.all_gather(vals_img, 'blk', axis=0, tiled=True)  26 us
    all_gather x1, waiting for transfers between devices, on_device(): lax.all_gather(w_out, 'req', axis=0, tiled=True)  13.5 us
    dot_general x1, matrix products, absorb_block(): jnp.einsum('qhd,khd->qhk', queries, head_keys, preferred_element_type=jnp...  8.82 us
    reduce_sum x1, other arithmetic, absorb_block(): jnp.sum(weights, axis=2)  7.21 us
    unnamed x30, local copies, waits for them, and re-layouts  5.57 us
  transfers between devices with their start and end apart: 7, of which 6 were waited for; matrix products, arithmetic and copies ran while one was open for 20% of the time, Pallas kernels for 0%

commit v1 on v0

--- a/solution.py
+++ b/solution.py
@@ -144,7 +144,12 @@
     tile_count = mask_row.shape[0]
     start_state = text_state(queries, keys_txt, vals_txt, length)
     piece_keys = lax.all_gather(keys_img, "blk", axis=0, tiled=True)
-    piece_vals = lax.all_gather(vals_img, "blk", axis=0, tiled=True)
+    ring = [vals_img]
+    for hop in range(3):
+        ring.append(lax.ppermute(ring[-1], "blk", [(dev, (dev + 1) % 4) for dev in range(4)]))
+    piece_vals = jnp.roll(
+        jnp.concatenate(ring[::-1], axis=0), (lax.axis_index("blk") + 1) * ring[0].shape[0], axis=0
+    )
     piece_len = piece_keys.shape[0]
     key_tile = jnp.arange(piece_len, dtype=jnp.int32) // tok_rows
     tile_hit = key_tile[:, None] == jnp.arange(tile_count, dtype=jnp.int32)[None, :]

time: 231 us -> 192 us (0.83)
  waiting for transfers between devices: 157 us -> 123 us
  matrix products: 28 us -> 22.2 us
  other arithmetic: 10.2 us -> 6.64 us
  starting transfers between devices: 4.88 us -> 7.72 us
    ppermute x0 -> x3, waiting for transfers between devices: none -> 35.2 us  [on_device(): lax.ppermute(ring[-1], 'blk', [(dev, (dev + 1) % 4) for dev in range(4)])]
    all_gather x1, waiting for transfers between devices: 30.4 us -> 0.02 us  [on_device(): lax.all_gather(w_txt, 'req', axis=1, tiled=True)]
    all_gather x1 -> x0, waiting for transfers between devices: 26 us -> none  [on_device(): piece_vals = lax.all_gather(vals_img, 'blk', axis=0, tiled=True)]
    all_gather x1, waiting for transfers between devices: 30.5 us -> 19.6 us  [on_device(): piece_keys = lax.all_gather(keys_img, 'blk', axis=0, tiled=True)]
    dot_general x1, matrix products: 8.82 us -> 4.23 us  [absorb_block(): jnp.einsum('qhd,khd->qhk', queries, head_keys, preferred_element_type=jnp...]
    reduce_sum x1, other arithmetic: 7.21 us -> 3.62 us  [absorb_block(): jnp.sum(weights, axis=2)]
    dynamic_slice x0 -> x2, local copies, waits for them, and re-layouts: none -> 3.16 us  [on_device(): jnp.roll(jnp.concatenate(ring[::-1], axis=0), (lax.axis_index('blk') + 1)...]
    ppermute x1, waiting for transfers between devices: 2.72 us -> 0.01 us  [with_halo(): lax.ppermute(lax.slice_in_dim(block, 0, width, axis=dim), axis, backward)]
  transfers between devices with their start and end apart: 7 -> 9, of which waited for: 6 -> 6; matrix products, arithmetic and copies ran while one was open for 20% -> 19% of each run, Pallas kernels for 0% -> 0%
where the time goes in v1:
time: 192 us; the launch traced here: 191 us
  waiting for transfers between devices  123 us (64%)
  matrix products  22.2 us (12%)
  local copies, waits for them, and re-layouts  15.6 us (8%)
  between operations  15.6 us (8%)
  starting transfers between devices  7.72 us (4%)
  other arithmetic  6.64 us (3%)
    all_gather x1, waiting for transfers between devices, on_device(): lax.all_gather(w_img, 'req', axis=1, tiled=True)  51.3 us
    ppermute x3, waiting for transfers between devices, on_device(): lax.ppermute(ring[-1], 'blk', [(dev, (dev + 1) % 4) for dev in range(4)])  35.2 us
    all_gather x1, waiting for transfers between devices, on_device(): piece_keys = lax.all_gather(keys_img, 'blk', axis=0, tiled=True)  19.6 us
    all_gather x1, waiting for transfers between devices, on_device(): lax.all_gather(w_out, 'req', axis=0, tiled=True)  15.6 us
    unnamed x39, local copies, waits for them, and re-layouts  6.14 us
    dot_general x1, matrix products, on_device(): jnp.dot(h_img, lax.all_gather(w_img, 'req', axis=1, tiled=True), preferre...  5.16 us
    ppermute x1, starting transfers between devices, with_halo(): lax.ppermute(lax.slice_in_dim(block, block.shape[dim] - width, None, axis...  4.55 us
    dot_general x1, matrix products, on_device(): jnp.dot(h_txt, lax.all_gather(w_txt, 'req', axis=1, tiled=True), preferre...  4.25 us
  transfers between devices with their start and end apart: 9, of which 6 were waited for; matrix products, arithmetic and copies ran while one was open for 19% of the time, Pallas kernels for 0%

profile of v1, /device:TPU:0, one launch (start us, length us, event | category | flops | bytes accessed | tf_op | source)
XLA Modules:
  0.0 191.2 jit_solution(7897881443088850206)
XLA Ops:
  7.2 0.0 copy-start
  7.2 0.0 all-gather.7.cloned.1.call-start
  7.2 0.7 all-gather.7.cloned.1.call-update
  7.9 0.0 all-gather.5.cloned.1.call-start
  8.0 0.7 all-gather.5.cloned.1.call-update
  8.7 0.0 all-gather.9.cloned.1.call-start
  8.7 0.9 add_reduce_fusion
  9.6 0.2 convert_reduce_fusion
  9.8 0.3 fusion.14
  10.2 51.3 %all-gather.7.cloned.1.call-done = bf16[1536,2304]{0,1:T(8,128)(2,1)} async-done(((bf16[1536,288]{0,1:T(8,128)(2,1)}), bf16[1536,2304]{0,1:T(8,128)(2,1)}) %all-gather.7.cloned.1.call-update) | async-done | bytes 7077904 | tf_op jit(solution)/shard_map/all_gather | solution.py:132
  61.5 5.2 %convolution_convert_fusion = bf16[256,2304]{1,0:T(8,128)(2,1)S(1)} fusion(bf16[1536,2304]{0,1:T(8,128)(2,1)} %all-gather.7.cloned.1.call-done, bf16[1,256,1536]{2,1,0:T(8,128)(2,1)S(1)} %copy-done.1, f32[1536]{0:T(1024)S(1)} %get-tuple-element.16, f32[1536]{0:T(1024)S(1)} %get-tuple-element.17, f32[256]{0:T(256)S(1)} %add_rsqrt_fusion.1, ...), kind=kOutput, calls=%fused_computation.10 | convolution fusion | flops 1814888448 | bytes 9058304 | tf_op jit(solution)/shard_map/dot_general | solution.py:131
  66.7 1.5 collective-permute-start
  68.2 11.6 %collective-permute-done = bf16[256,768]{1,0:T(8,128)(2,1)S(1)} collective-permute-done((bf16[256,768]{1,0:T(8,128)(2,1)S(1)}, bf16[256,768]{1,0:T(8,128)(2,1)S(1)}, u32[]{:S(2)}, u32[]{:S(2)}) %collective-permute-start) | collective-permute-done | bytes 393248 | tf_op jit(solution)/shard_map/ppermute | solution.py:149
  79.8 0.0 collective-permute-start.1
  79.8 12.3 %collective-permute-done.1 = bf16[256,768]{1,0:T(8,128)(2,1)S(1)} collective-permute-done((bf16[256,768]{1,0:T(8,128)(2,1)S(1)}, bf16[256,768]{1,0:T(8,128)(2,1)S(1)}, u32[]{:S(2)}, u32[]{:S(2)}) %collective-permute-start.1) | collective-permute-done | bytes 393248 | tf_op jit(solution)/shard_map/ppermute | solution.py:149
  92.1 11.3 %collective-permute-done.2 = bf16[256,768]{1,0:T(8,128)(2,1)S(1)} collective-permute-done((bf16[256,768]{1,0:T(8,128)(2,1)S(1)}, bf16[256,768]{1,0:T(8,128)(2,1)S(1)}, u32[]{:S(2)}, u32[]{:S(2)}) %collective-permute-start.2) | collective-permute-done | bytes 393248 | tf_op jit(solution)/shard_map/ppermute | solution.py:149
  103.6 0.0 copy-start.9
  103.7 0.0 copy-start.3
  103.7 0.0 copy-start.8
  103.7 0.8 fusion.69
  104.5 1.7 copy-done.5
  106.2 0.0 all-gather.9.cloned.1.call-update
  106.2 0.2 all-gather.11.cloned.1.call-start
  106.5 0.3 all-gather.11.cloned.1.call-update
  107.5 0.1 select_reduce_fusion
  108.3 0.1 convert_reduce_fusion.1
  108.4 0.3 fusion.30
  108.7 1.0 copy.65
  109.8 0.0 all-gather.5.cloned.1.call-done
  109.9 4.3 %convolution_convert_fusion.1 = bf16[154,1536]{1,0:T(8,128)(2,1)S(1)} fusion(bf16[1536,1536]{0,1:T(8,128)(2,1)} %all-gather.5.cloned.1.call-done, bf16[1,154,1536]{2,1,0:T(8,128)(2,1)S(1)} %copy-done.3, f32[1536]{0:T(1024)S(1)} %get-tuple-element.18, f32[1536]{0:T(1024)S(1)} %get-tuple-element.19, f32[154]{0:T(256)S(1)} %add_rsqrt_fusion.2, ...), kind=kOutput, calls=%fused_computation.13 | convolution fusion | flops 728318976 | bytes 5678288 | tf_op jit(solution)/shard_map/dot_general | solution.py:134
  114.2 0.9 copy.59
  115.1 0.9 copy.58
  116.0 1.5 constant_dynamic-slice_fusion
  117.5 1.7 copy.62
  119.2 0.2 copy.60
  119.3 1.6 bitcast_reduce_fusion.1
  120.9 0.6 fusion.18
  121.5 19.6 %all-gather.9.cloned.1.call-done = bf16[1024,768]{1,0:T(8,128)(2,1)} async-done(((bf16[256,768]{1,0:T(8,128)(2,1)}), bf16[1024,768]{1,0:T(8,128)(2,1)}) %all-gather.9.cloned.1.call-update) | async-done | bytes 1572880 | tf_op jit(solution)/shard_map/all_gather | solution.py:146
  141.0 2.6 %copy.61 = bf16[1024,768]{0,1:T(8,128)(2,1)} copy(bf16[1024,768]{1,0:T(8,128)(2,1)} %all-gather.9.cloned.1.call-done) | data formatting | bytes 3145728 | tf_op jit(solution)/shard_map/all_gather | solution.py:146
  143.6 4.2 %bitcast_reduce_fusion = (f32[256,12]{0,1:T(8,128)S(1)}, f32[12,1024,256]{2,1,0:T(8,128)S(1)}) fusion(pred[1024]{0:T(1024)(128)(4,1)S(1)} %broadcast_compare_fusion, bf16[1024,12,64]{0,2,1:T(8,128)(2,1)} %bitcast.129, bf16[256,12,64]{0,2,1:T(8,128)(2,1)S(1)} %bitcast.134), kind=kOutput, calls=%fused_computation.1 | convolution fusion | flops 412087296 | bytes 14562304 | tf_op jit(solution)/shard_map/qhd,khd->qhk/dot_general | solution.py:89
  147.9 3.6 %fusion.2 = f32[256,12]{0,1:T(8,128)S(1)} fusion(f32[12,1024,256]{2,1,0:T(8,128)S(1)} %get-tuple-element.45, f32[256,12]{0,1:T(8,128)S(1)} %max.13, pred[1024]{0:T(1024)(128)(4,1)S(1)} %broadcast_compare_fusion), kind=kLoop, calls=%fused_computation.5 | loop fusion | flops 15725568 | bytes 12608512 | tf_op jit(solution)/shard_map/reduce_sum | solution.py:101
  151.6 2.8 %fusion.20 = f32[256,12,64]{0,2,1:T(8,128)S(1)} fusion(bf16[1024,12,64]{0,2,1:T(8,128)(2,1)S(1)} %bitcast.135, f32[12,1024,256]{2,1,0:T(8,128)S(1)} %get-tuple-element.45, f32[256,12]{0,1:T(8,128)S(1)} %max.13, pred[1024]{0:T(1024)(128)(4,1)S(1)} %broadcast_compare_fusion), kind=kOutput, calls=%fused_computation.33 | convolution fusion | flops 418381824 | bytes 14955520 | tf_op jit(solution)/shard_map/qhk,khd->qhd/dot_general | solution.py:96
  154.4 0.7 fusion.26
  155.1 15.6 %all-gather.11.cloned.1.call-done = bf16[768,1536]{1,0:T(8,128)(2,1)} async-done(((bf16[96,1536]{1,0:T(8,128)(2,1)}), bf16[768,1536]{1,0:T(8,128)(2,1)}) %all-gather.11.cloned.1.call-update) | async-done | bytes 2359312 | tf_op jit(solution)/shard_map/all_gather | solution.py:165
  170.7 2.5 %fusion.72 = (f32[256]{0:T(256)S(1)}, f32[256,1536]{1,0:T(8,128)S(1)}) fusion(bf16[256,768]{0,1:T(8,128)(2,1)S(1)} %bitcast.137, bf16[768,1536]{1,0:T(8,128)(2,1)} %all-gather.11.cloned.1.call-done, f32[1536]{0:T(1024)S(1)} %get-tuple-element.20, bf16[1,256,1536]{2,1,0:T(8,128)(2,1)S(1)} %copy-done.1), kind=kOutput, calls=%fused_computation.136 | convolution fusion | flops 605552384 | bytes 5118976 | tf_op jit(solution)/shard_map/dot_general | solution.py:163
  173.2 0.0 copy-start.2
  173.3 0.3 multiply_reduce_fusion
  173.6 0.5 fusion.46
  174.1 0.1 reshape.190
  174.2 0.3 copy.64
  174.5 0.0 copy-start.7
  174.5 0.1 add_convert_fusion.2
  174.6 1.3 collective-permute-start.4
  175.9 4.5 %collective-permute-start.3 = (bf16[1,16,1,128]{1,3,2,0:T(8,128)(2,1)S(1)}, bf16[1,16,1,128]{1,3,2,0:T(8,128)(2,1)S(1)}, u32[]{:S(2)}, u32[]{:S(2)}) collective-permute-start(bf16[1,16,1,128]{1,3,2,0:T(8,128)(2,1)S(1)} %get-tuple-element.31), channel_id=1, source_target_pairs={{0,1},{1,2},{2,3},{4,5},{5,6},{6,7},{8,9},{9,10},{10,11},{12,13},{... | collective-permute-start | bytes 12296 | tf_op jit(solution)/shard_map/ppermute | solution.py:24
  180.5 0.8 copy.78
  181.3 0.1 copy.67
  181.4 0.8 copy.79
  182.2 0.0 collective-permute-done.4
  182.2 0.1 copy.68
  182.2 0.0 collective-permute-done.3
  182.2 0.1 copy.66
  182.4 0.1 fusion.59
  182.7 0.5 convolution_convert_fusion.2
  183.2 1.5 copy.80
  (45 shorter events, 0.6 us)
Async XLA Ops:
  7.2 166.4 %copy-start = (bf16[1536,64]{0,1:T(8,128)(2,1)S(1)}, bf16[1536,64]{0,1:T(8,128)(2,1)}, u32[]{:S(2)}) copy-start(bf16[1536,64]{0,1:T(8,128)(2,1)} %param.18) | copy-start | bytes 589828
  7.2 2.5 %copy-start.1 = (bf16[1,256,1536]{2,1,0:T(8,128)(2,1)S(1)}, bf16[1,256,1536]{2,1,0:T(8,128)(2,1)}, u32[]{:S(2)}) copy-start(bf16[1,256,1536]{2,1,0:T(8,128)(2,1)} %param.12) | copy-start | bytes 2359300
  7.2 54.3 %all-gather.7.cloned.1.call-start = ((), (), s32[]{:S(2)}) async-start(), calls=%async_computation.1 | async-start | bytes 7962624 | tf_op jit(solution)/shard_map/all_gather | solution.py:132
  7.9 101.9 %all-gather.5.cloned.1.call-start = ((), (), s32[]{:S(2)}) async-start(), calls=%async_computation | async-start | bytes 5308416 | tf_op jit(solution)/shard_map/all_gather | solution.py:135
  8.7 132.4 %all-gather.9.cloned.1.call-start = ((), (), s32[]{:S(2)}) async-start(), calls=%async_computation.2 | async-start | bytes 1966080 | tf_op jit(solution)/shard_map/all_gather | solution.py:146
  66.7 13.1 %collective-permute-start = (bf16[256,768]{1,0:T(8,128)(2,1)S(1)}, bf16[256,768]{1,0:T(8,128)(2,1)S(1)}, u32[]{:S(2)}, u32[]{:S(2)}) collective-permute-start(bf16[256,768]{1,0:T(8,128)(2,1)S(1)} %slice.106), channel_id=1, source_target_pairs={{0,1},{1,2},{2,3},{3,0},{4,5},{5,6},{6,7},{7,4},{8,9},{9,10},{10,1... | collective-permute-start | bytes 1179656 | tf_op jit(solution)/shard_map/ppermute | solution.py:149
  79.8 12.3 %collective-permute-start.1 = (bf16[256,768]{1,0:T(8,128)(2,1)S(1)}, bf16[256,768]{1,0:T(8,128)(2,1)S(1)}, u32[]{:S(2)}, u32[]{:S(2)}) collective-permute-start(bf16[256,768]{1,0:T(8,128)(2,1)S(1)} %collective-permute-done), channel_id=1, source_target_pairs={{0,1},{1,2},{2,3},{3,0},{4,5},{5,6},{6,7},{7,4},{8,9},{9,10},{10,1... | collective-permute-start | bytes 1179656 | tf_op jit(solution)/shard_map/ppermute | solution.py:149
  92.1 11.3 %collective-permute-start.2 = (bf16[256,768]{1,0:T(8,128)(2,1)S(1)}, bf16[256,768]{1,0:T(8,128)(2,1)S(1)}, u32[]{:S(2)}, u32[]{:S(2)}) collective-permute-start(bf16[256,768]{1,0:T(8,128)(2,1)S(1)} %collective-permute-done.1), channel_id=1, source_target_pairs={{0,1},{1,2},{2,3},{3,0},{4,5},{5,6},{6,7},{7,4},{8,9},{9,10},{10,1... | collective-permute-start | bytes 1179656 | tf_op jit(solution)/shard_map/ppermute | solution.py:149
  103.6 3.9 %copy-start.9 = (s32[1,1,4]{2,1,0:T(1,128)S(1)}, s32[1,1,4]{2,1,0:T(1,128)}, u32[]{:S(2)}) copy-start(s32[1,1,4]{2,1,0:T(1,128)} %param.20) | copy-start | bytes 52
  103.7 4.6 %copy-start.3 = (bf16[1,154,1536]{2,1,0:T(8,128)(2,1)S(1)}, bf16[1,154,1536]{2,1,0:T(8,128)(2,1)}, u32[]{:S(2)}) copy-start(bf16[1,154,1536]{2,1,0:T(8,128)(2,1)} %param.13) | copy-start | bytes 1419268
  103.7 5.0 %copy-start.8 = (f32[1,16,8,128]{3,2,1,0:T(8,128)S(1)}, f32[1,16,8,128]{3,2,1,0:T(8,128)}, u32[]{:S(2)}) copy-start(f32[1,16,8,128]{3,2,1,0:T(8,128)} %param.22) | copy-start | bytes 196612
  104.5 1.7 copy-start.5
  106.2 64.5 %all-gather.11.cloned.1.call-start = ((), (), s32[]{:S(2)}) async-start(), calls=%async_computation.3 | async-start | bytes 2654208 | tf_op jit(solution)/shard_map/all_gather | solution.py:165
  147.9 3.7 %copy-start.4 = (bf16[1024,768]{0,1:T(8,128)(2,1)S(1)}, bf16[1024,768]{0,1:T(8,128)(2,1)}, u32[]{:S(2)}) copy-start(bf16[1024,768]{0,1:T(8,128)(2,1)} %copy.62) | copy-start | bytes 4718596
  151.6 2.8 %copy-start.6 = (bf16[154,768]{0,1:T(8,128)(2,1)S(1)}, bf16[154,768]{0,1:T(8,128)(2,1)}, u32[]{:S(2)}) copy-start(bf16[154,768]{0,1:T(8,128)(2,1)} %copy.58) | copy-start | bytes 709636
  173.2 1.2 copy-start.2
  174.5 8.3 %copy-start.7 = (bf16[512,144]{0,1:T(8,128)(2,1)S(1)}, bf16[512,144]{0,1:T(8,128)(2,1)}, u32[]{:S(2)}) copy-start(bf16[512,144]{0,1:T(8,128)(2,1)} %param.23) | copy-start | bytes 442372
  174.6 7.6 %collective-permute-start.4 = (bf16[1,16,1,128]{1,3,2,0:T(8,128)(2,1)S(1)}, bf16[1,16,1,128]{1,3,2,0:T(8,128)(2,1)S(1)}, u32[]{:S(2)}, u32[]{:S(2)}) collective-permute-start(bf16[1,16,1,128]{1,3,2,0:T(8,128)(2,1)S(1)} %get-tuple-element.32), channel_id=1, source_target_pairs={{1,0},{2,1},{3,2},{5,4},{6,5},{7,6},{9,8},{10,9},{11,10},{13,12},{... | collective-permute-start | bytes 12296 | tf_op jit(solution)/shard_map/ppermute | solution.py:27
  175.9 6.3 %collective-permute-start.3 = (bf16[1,16,1,128]{1,3,2,0:T(8,128)(2,1)S(1)}, bf16[1,16,1,128]{1,3,2,0:T(8,128)(2,1)S(1)}, u32[]{:S(2)}, u32[]{:S(2)}) collective-permute-start(bf16[1,16,1,128]{1,3,2,0:T(8,128)(2,1)S(1)} %get-tuple-element.31), channel_id=1, source_target_pairs={{0,1},{1,2},{2,3},{4,5},{5,6},{6,7},{8,9},{9,10},{10,11},{12,13},{... | collective-permute-start | bytes 12296 | tf_op jit(solution)/shard_map/ppermute | solution.py:24
Sparse Core Ops, SparseCore 0:
  9.9 51.5 all-gather.6
  63.4 38.9 all-gather.4
  106.3 34.6 all-gather.8
  142.8 27.8 all-gather.10
